TPU v7x, 128 devices: a whole 4x4x4 slice. The times are simulated.
128 devices in a mesh: wide: 16 (over z, x), narrow: 8 (over y, core).
Axes of the slice: x: 4, y: 4, z: 4, core: 2. Of those that a mesh axis runs over, the one named last changes fastest.
Arguments:
- coeffs: float32 [24, 64, 131072], P(None, None, ('wide', 'narrow')), may hold values from -6 to 6
- phases: float32 [6, 24, 131072], P(None, None, ('wide', 'narrow')), may hold values from -3.140625 to 3.140625
- mixers: float32 [6, 2, 2, 24, 24], replicated, may hold values from -1.25 to 1.25
Outputs:
- result: float32 [24, 64, 131072], P(None, None, ('wide', 'narrow'))
All inputs are finite; a program needn't handle non-finite values.
Results may differ from a plain program's by a relative error of at most 0.0003.
Values sent between devices are 32-bit elements; how exact they have to be, the bound alone decides.
A program may use at most 128 MiB of HBM per device.

v0:
```python
import jax
import jax.numpy as jnp
from jax import lax
from jax.sharding import PartitionSpec as P


def swapped(shard, axis, distance):
    return lax.ppermute(shard, axis, [(i, i ^ 1 << distance) for i in range(lax.axis_size(axis))])


def combine_level(field, angle, mixing, position):
    rank_size, col_size, total = field.shape
    low = 2**position
    shaped = field.reshape(rank_size, col_size, total // (2 * low), 2, low)
    angled = angle.reshape(rank_size, total // (2 * low), 2, low)
    first = shaped[:, :, :, 0, :]
    second = shaped[:, :, :, 1, :]
    outputs = []
    for side in range(2):
        summed = jnp.einsum(
            "ar,rcbk->acbk", mixing[side, 0], first, precision=lax.Precision.HIGHEST
        )
        summed = summed + jnp.einsum(
            "ar,rcbk->acbk", mixing[side, 1], second, precision=lax.Precision.HIGHEST
        )
        outputs.append(jnp.cos(angled[:, :, side, :])[:, None, :, :] * summed)
    return jnp.stack(outputs, axis=3).reshape(rank_size, col_size, total)


def paired_level(field, partner, angle, mixing, side):
    own_part = jnp.einsum("ar,rcb->acb", mixing[side, side], field, precision=lax.Precision.HIGHEST)
    other_part = jnp.einsum(
        "ar,rcb->acb", mixing[side, 1 - side], partner, precision=lax.Precision.HIGHEST
    )
    return jnp.cos(angle)[:, None, :] * (own_part + other_part)


def on_device(coeffs, phases, mixers):
    rank_size, col_size, blocks = coeffs.shape
    log_near = lax.axis_size("narrow").bit_length() - 1
    log_wide = lax.axis_size("wide").bit_length() - 1
    field = coeffs
    near_bits = [0, log_near - 1]
    for level in range(2):
        partner = swapped(field, "narrow", near_bits[level])
        side = lax.axis_index("narrow") >> near_bits[level] & 1
        field = paired_level(field, partner, phases[level], mixers[level], side)
    field = combine_level(field, phases[2], mixers[2], blocks.bit_length() - 2)
    for level in range(3):
        wide_bit = log_wide - 3 + level
        partner = swapped(field, "wide", wide_bit)
        side = lax.axis_index("wide") >> wide_bit & 1
        field = paired_level(field, partner, phases[3 + level], mixers[3 + level], side)
    return field


def solution(mesh):
    placed = (P(None, None, ("wide", "narrow")), P(None, None, ("wide", "narrow")), P())
    return jax.shard_map(
        on_device,
        mesh=mesh,
        in_specs=placed,
        out_specs=P(None, None, ("wide", "narrow")),
        check_vma=False,
    )
```

profile of v0, /device:TPU:0, one launch (start us, length us, event | category | flops | bytes accessed | tf_op | source)
XLA Modules:
  0.0 687.4 jit_solution(17251797680183521585)
XLA Ops:
  0.0 0.0 copy-start.2
  0.0 0.0 copy-start.1
  0.0 9.2 %copy.12 = f32[24,64,1024]{2,0,1:T(8,128)} copy(f32[24,64,1024]{2,1,0:T(8,128)} %param.3) | data formatting | bytes 12582912 | tf_op args[0]
  9.2 0.3 collective-permute-start
  9.5 0.0 copy-done.2
  9.5 0.7 fusion.45
  10.2 0.0 copy-done.1
  10.2 1.5 cosine_bitcast_fusion.4
  11.8 12.2 %fusion.13 = f32[24,64,1024]{2,0,1:T(8,128)S(1)} fusion(f32[1,2,2,24,24]{4,3,2,1,0:T(8,128)S(1)} %get-tuple-element.18, s32[]{:T(128)S(6)} %select_n.44, f32[24,64,1024]{2,1,0:T(8,128)} %param.3), kind=kOutput, calls=%fused_computation.35 | convolution fusion | flops 452984832 | bytes 12595204 | tf_op jit(solution)/shard_map/ar,rcb->acb/dot_general | solution.py:31
  24.0 0.0 collective-permute-done
  24.0 9.4 %add_multiply_fusion.4 = f32[24,64,1024]{2,0,1:T(8,128)} fusion(f32[24,64,1024]{2,0,1:T(8,128)S(1)} %fusion.13, f32[24,1024]{1,0:T(8,128)S(1)} %get-tuple-element.11, f32[24,64,1024]{2,0,1:T(8,128)} %collective-permute-done, f32[1,2,2,24,24]{4,3,2,1,0:T(8,128)S(1)} %get-tuple-element.18, s32[]{:T(128)S(6)} %select_n.44, s32[]{:T(128)S(6)} %select_n.45), kind=kOutput, calls=%fused_computation.5 | convolution fusion | flops 456130560 | bytes 18984968 | tf_op jit(solution)/shard_map/ar,rcb->acb/dot_general | solution.py:32
  33.4 3.8 collective-permute-start.1
  37.2 0.1 reshape_squeeze.3
  37.3 0.1 fusion.46
  37.4 0.3 fusion.6
  37.7 8.2 %fusion.15 = f32[24,64,1024]{2,0,1:T(8,128)S(1)} fusion(f32[24,64,1024]{2,0,1:T(8,128)} %add_multiply_fusion.4, f32[1,2,2,24,24]{4,3,2,1,0:T(8,128)S(1)} %get-tuple-element.14, s32[]{:T(128)S(6)} %select_n.43), kind=kOutput, calls=%fused_computation.37 | convolution fusion | flops 452984832 | bytes 12595204 | tf_op jit(solution)/shard_map/ar,rcb->acb/dot_general | solution.py:31
  45.9 127.8 %collective-permute-done.1 = f32[24,64,1024]{2,0,1:T(8,128)} collective-permute-done((f32[24,64,1024]{2,0,1:T(8,128)}, f32[24,64,1024]{2,0,1:T(8,128)}, u32[]{:S(2)}, u32[]{:S(2)}) %collective-permute-start.1) | collective-permute-done | bytes 6291488 | tf_op jit(solution)/shard_map/ppermute | solution.py:8
  173.7 9.4 %add_multiply_fusion.3 = f32[24,64,1024]{2,0,1:T(8,128)} fusion(f32[24,64,1024]{2,0,1:T(8,128)S(1)} %fusion.15, f32[24,1024]{1,0:T(8,128)S(1)} %get-tuple-element.12, f32[24,64,1024]{2,0,1:T(8,128)} %collective-permute-done.1, f32[1,2,2,24,24]{4,3,2,1,0:T(8,128)S(1)} %get-tuple-element.14, s32[]{:T(128)S(6)} %select_n.43, s32[]{:T(128)S(6)} %select_n.46), kind=kOutput, calls=%fused_computation.4 | convolution fusion | flops 456130560 | bytes 18984968 | tf_op jit(solution)/shard_map/ar,rcb->acb/dot_general | solution.py:32
  183.1 9.3 %reshape.88 = f32[24,64,1,2,512]{4,3,0,1,2:T(2,128)} reshape(f32[24,64,1024]{2,0,1:T(8,128)} %add_multiply_fusion.3) | data formatting | bytes 12582912 | tf_op jit(solution)/shard_map/reshape | solution.py:14
  192.5 12.9 %fusion.44 = (f32[24,64,1,1,512]{4,3,0,1,2:T(1,128)S(1)}, f32[24,64,1,1,512]{4,3,0,1,2:T(1,128)}) fusion(f32[24,64,1,2,512]{4,3,0,1,2:T(2,128)} %reshape.88), kind=kLoop, calls=%fused_computation.66 | loop fusion | bytes 12582912 | tf_op jit(solution)/shard_map/slice | solution.py:17
  205.3 0.0 copy-start
  205.3 0.0 copy-start.3
  205.3 5.4 fusion.3
  210.8 0.0 copy-done
  210.8 0.0 copy-done.3
  210.8 3.6 fusion.2
  214.4 3.5 fusion.1
  218.0 3.5 fusion
  221.5 0.7 pad_maximum_fusion
  222.2 8.5 %copy.21 = f32[24,64,1,2,512]{4,3,0,1,2:T(2,128)} copy(f32[24,64,1,2,512]{4,0,1,3,2:T(8,128)S(1)} %pad_maximum_fusion) | data formatting | bytes 12582912 | tf_op jit(solution)/shard_map/reshape | solution.py:27
  230.8 9.2 %reshape.106 = f32[24,64,1024]{2,0,1:T(8,128)} reshape(f32[24,64,1,2,512]{4,3,0,1,2:T(2,128)} %copy.21) | data formatting | bytes 12582912 | tf_op jit(solution)/shard_map/reshape | solution.py:27
  240.0 3.1 collective-permute-start.2
  243.1 0.0 copy-done.6
  243.1 8.2 %fusion.17 = f32[24,64,1024]{2,0,1:T(8,128)S(1)} fusion(f32[24,64,1024]{2,0,1:T(8,128)} %reshape.106, f32[1,2,2,24,24]{4,3,2,1,0:T(8,128)S(1)} %copy-done.6, s32[]{:T(128)S(6)} %select_n.42), kind=kOutput, calls=%fused_computation.39 | convolution fusion | flops 452984832 | bytes 12595204 | tf_op jit(solution)/shard_map/ar,rcb->acb/dot_general | solution.py:31
  251.3 127.7 %collective-permute-done.2 = f32[24,64,1024]{2,0,1:T(8,128)} collective-permute-done((f32[24,64,1024]{2,0,1:T(8,128)}, f32[24,64,1024]{2,0,1:T(8,128)}, u32[]{:S(2)}, u32[]{:S(2)}) %collective-permute-start.2) | collective-permute-done | bytes 6291488 | tf_op jit(solution)/shard_map/ppermute | solution.py:8
  379.0 0.0 copy-start.5
  379.0 9.4 %add_multiply_fusion.2 = f32[24,64,1024]{2,0,1:T(8,128)} fusion(f32[24,64,1024]{2,0,1:T(8,128)S(1)} %fusion.17, f32[24,1024]{1,0:T(8,128)S(1)} %get-tuple-element.9, f32[24,64,1024]{2,0,1:T(8,128)} %collective-permute-done.2, f32[1,2,2,24,24]{4,3,2,1,0:T(8,128)S(1)} %copy-done.6, s32[]{:T(128)S(6)} %select_n.42, s32[]{:T(128)S(6)} %select_n.47), kind=kOutput, calls=%fused_computation.3 | convolution fusion | flops 456130560 | bytes 18984968 | tf_op jit(solution)/shard_map/ar,rcb->acb/dot_general | solution.py:32
  388.4 1.9 collective-permute-start.3
  390.4 0.0 copy-done.5
  390.4 8.2 %fusion.19 = f32[24,64,1024]{2,0,1:T(8,128)S(1)} fusion(f32[24,64,1024]{2,0,1:T(8,128)} %add_multiply_fusion.2, f32[1,2,2,24,24]{4,3,2,1,0:T(8,128)S(1)} %copy-done.5, s32[]{:T(128)S(6)} %select_n.41), kind=kOutput, calls=%fused_computation.41 | convolution fusion | flops 452984832 | bytes 12595204 | tf_op jit(solution)/shard_map/ar,rcb->acb/dot_general | solution.py:31
  398.6 126.6 %collective-permute-done.3 = f32[24,64,1024]{2,0,1:T(8,128)} collective-permute-done((f32[24,64,1024]{2,0,1:T(8,128)}, f32[24,64,1024]{2,0,1:T(8,128)}, u32[]{:S(2)}, u32[]{:S(2)}) %collective-permute-start.3) | collective-permute-done | bytes 6291488 | tf_op jit(solution)/shard_map/ppermute | solution.py:8
  525.2 9.4 %add_multiply_fusion.1 = f32[24,64,1024]{2,0,1:T(8,128)} fusion(f32[24,64,1024]{2,0,1:T(8,128)S(1)} %fusion.19, f32[24,1024]{1,0:T(8,128)S(1)} %get-tuple-element.10, f32[24,64,1024]{2,0,1:T(8,128)} %collective-permute-done.3, f32[1,2,2,24,24]{4,3,2,1,0:T(8,128)S(1)} %copy-done.5, s32[]{:T(128)S(6)} %select_n.41, s32[]{:T(128)S(6)} %select_n.48), kind=kOutput, calls=%fused_computation.2 | convolution fusion | flops 456130560 | bytes 18984968 | tf_op jit(solution)/shard_map/ar,rcb->acb/dot_general | solution.py:32
  534.6 3.7 collective-permute-start.4
  538.3 0.0 copy-done.4
  538.3 8.4 %fusion.21 = f32[24,64,1024]{2,0,1:T(8,128)S(1)} fusion(f32[24,64,1024]{2,0,1:T(8,128)} %add_multiply_fusion.1, f32[1,2,2,24,24]{4,3,2,1,0:T(8,128)S(1)} %copy-done.4, s32[]{:T(128)S(6)} %select_n.40), kind=kOutput, calls=%fused_computation.43 | convolution fusion | flops 452984832 | bytes 12595204 | tf_op jit(solution)/shard_map/ar,rcb->acb/dot_general | solution.py:31
  546.7 125.5 %collective-permute-done.4 = f32[24,64,1024]{2,0,1:T(8,128)} collective-permute-done((f32[24,64,1024]{2,0,1:T(8,128)}, f32[24,64,1024]{2,0,1:T(8,128)}, u32[]{:S(2)}, u32[]{:S(2)}) %collective-permute-start.4) | collective-permute-done | bytes 6291488 | tf_op jit(solution)/shard_map/ppermute | solution.py:8
  672.1 8.7 %add_multiply_fusion = f32[24,64,1024]{2,0,1:T(8,128)S(1)} fusion(f32[24,64,1024]{2,0,1:T(8,128)S(1)} %fusion.21, f32[24,1024]{1,0:T(8,128)S(1)} %get-tuple-element.7, f32[24,64,1024]{2,0,1:T(8,128)} %collective-permute-done.4, f32[1,2,2,24,24]{4,3,2,1,0:T(8,128)S(1)} %copy-done.4, s32[]{:T(128)S(6)} %select_n.40, s32[]{:T(128)S(6)} %select_n.49), kind=kOutput, calls=%fused_computation.1 | convolution fusion | flops 456130560 | bytes 18984968 | tf_op jit(solution)/shard_map/ar,rcb->acb/dot_general | solution.py:32
  680.9 6.3 copy.20
  (2 shorter events, 0.0 us)
Async XLA Ops:
  0.0 9.5 %copy-start.2 = (f32[6,2,2,24,24]{4,3,2,1,0:T(8,128)S(1)}, f32[6,2,2,24,24]{4,3,2,1,0:T(8,128)}, u32[]{:S(2)}) copy-start(f32[6,2,2,24,24]{4,3,2,1,0:T(8,128)} %param.5) | copy-start | bytes 165892
  0.0 10.2 %copy-start.1 = (f32[6,24,1024]{2,1,0:T(8,128)S(1)}, f32[6,24,1024]{2,1,0:T(8,128)}, u32[]{:S(2)}) copy-start(f32[6,24,1024]{2,1,0:T(8,128)} %param.4) | copy-start | bytes 1769476
  9.2 14.8 %collective-permute-start = (f32[24,64,1024]{2,0,1:T(8,128)}, f32[24,64,1024]{2,0,1:T(8,128)}, u32[]{:S(2)}, u32[]{:S(2)}) collective-permute-start(f32[24,64,1024]{2,0,1:T(8,128)} %copy.12), channel_id=1, source_target_pairs={{0,1},{1,0},{2,3},{3,2},{4,5},{5,4},{6,7},{7,6},{8,9},{9,8},{10,11... | collective-permute-start | bytes 18874376 | tf_op jit(solution)/shard_map/ppermute | solution.py:8
  33.4 140.3 %collective-permute-start.1 = (f32[24,64,1024]{2,0,1:T(8,128)}, f32[24,64,1024]{2,0,1:T(8,128)}, u32[]{:S(2)}, u32[]{:S(2)}) collective-permute-start(f32[24,64,1024]{2,0,1:T(8,128)} %add_multiply_fusion.4), channel_id=1, source_target_pairs={{0,4},{1,5},{2,6},{3,7},{4,0},{5,1},{6,2},{7,3},{8,12},{9,13},{10,... | collective-permute-start | bytes 18874376 | tf_op jit(solution)/shard_map/ppermute | solution.py:8
  205.3 5.4 copy-start
  205.3 5.5 copy-start.3
  230.8 12.3 %copy-start.6 = (f32[1,2,2,24,24]{4,3,2,1,0:T(8,128)S(1)}, f32[1,2,2,24,24]{4,3,2,1,0:T(8,128)}, u32[]{:S(2)}) copy-start(f32[1,2,2,24,24]{4,3,2,1,0:T(8,128)} %get-tuple-element.15) | copy-start | bytes 27652
  240.0 139.0 %collective-permute-start.2 = (f32[24,64,1024]{2,0,1:T(8,128)}, f32[24,64,1024]{2,0,1:T(8,128)}, u32[]{:S(2)}, u32[]{:S(2)}) collective-permute-start(f32[24,64,1024]{2,0,1:T(8,128)} %reshape.106), channel_id=1, source_target_pairs={{0,16},{8,24},{16,0},{24,8},{32,48},{40,56},{48,32},{56,40},{64,80... | collective-permute-start | bytes 18874376 | tf_op jit(solution)/shard_map/ppermute | solution.py:8
  379.0 11.4 %copy-start.5 = (f32[1,2,2,24,24]{4,3,2,1,0:T(8,128)S(1)}, f32[1,2,2,24,24]{4,3,2,1,0:T(8,128)}, u32[]{:S(2)}) copy-start(f32[1,2,2,24,24]{4,3,2,1,0:T(8,128)} %get-tuple-element.16) | copy-start | bytes 27652
  388.4 136.8 %collective-permute-start.3 = (f32[24,64,1024]{2,0,1:T(8,128)}, f32[24,64,1024]{2,0,1:T(8,128)}, u32[]{:S(2)}, u32[]{:S(2)}) collective-permute-start(f32[24,64,1024]{2,0,1:T(8,128)} %add_multiply_fusion.2), channel_id=1, source_target_pairs={{0,32},{8,40},{16,48},{24,56},{32,0},{40,8},{48,16},{56,24},{64,96... | collective-permute-start | bytes 18874376 | tf_op jit(solution)/shard_map/ppermute | solution.py:8
  525.2 13.1 %copy-start.4 = (f32[1,2,2,24,24]{4,3,2,1,0:T(8,128)S(1)}, f32[1,2,2,24,24]{4,3,2,1,0:T(8,128)}, u32[]{:S(2)}) copy-start(f32[1,2,2,24,24]{4,3,2,1,0:T(8,128)} %get-tuple-element.13) | copy-start | bytes 27652
  534.6 137.5 %collective-permute-start.4 = (f32[24,64,1024]{2,0,1:T(8,128)}, f32[24,64,1024]{2,0,1:T(8,128)}, u32[]{:S(2)}, u32[]{:S(2)}) collective-permute-start(f32[24,64,1024]{2,0,1:T(8,128)} %add_multiply_fusion.1), channel_id=1, source_target_pairs={{0,64},{8,72},{16,80},{24,88},{32,96},{40,104},{48,112},{56,120},{... | collective-permute-start | bytes 18874376 | tf_op jit(solution)/shard_map/ppermute | solution.py:8
where the time goes:
time: 691 us; the launch traced here: 687 us
  waiting for transfers between devices  508 us (74%)
  matrix products  108 us (16%)
  local copies, waits for them, and re-layouts  58.3 us (8%)
  starting transfers between devices  12.7 us (2%)
    ppermute x5, waiting for transfers between devices, swapped(): lax.ppermute(shard, axis, [(i, i ^ 1 << distance) for i in range(lax.axis...  508 us
    dot_general x5, matrix products, paired_level(): jnp.einsum('ar,rcb->acb', mixing[side, 1 - side], partner, precision=lax....  46.4 us
    dot_general x5, matrix products, paired_level(): jnp.einsum('ar,rcb->acb', mixing[side, side], field, precision=lax.Precis...  45.2 us
    reshape x2, local copies, waits for them, and re-layouts, combine_level(): return jnp.stack(outputs, axis=3).reshape(rank_size, col_size, total)  17.8 us
  transfers between devices with their start and end apart: 5, of which 4 were waited for; matrix products, arithmetic and copies ran while one was open for 7% of the time, Pallas kernels for 0%

commit v1 on v0

v1 whole, which is shorter than its diff:
```python
import functools

import jax
import jax.numpy as jnp
from jax import lax
from jax.experimental import pallas as pl
from jax.experimental.pallas import tpu as pltpu
from jax.sharding import PartitionSpec as P

MESH = pl.DeviceIdType.MESH
SUB = 8
SPLITS = 2
WIDTH = 256 // SPLITS


def split(x):
    high = x.astype(jnp.bfloat16)
    return high, (x - high.astype(jnp.float32)).astype(jnp.bfloat16)


def mixed(w, own, other):
    rows = own.shape[0]
    own_high, own_low = split(own)
    other_high, other_low = split(other)
    high = jnp.concatenate([own_high, other_high], axis=0)
    low = jnp.concatenate([own_low, other_low], axis=0)
    both = jnp.dot(w[...], high, preferred_element_type=jnp.float32)
    rest = jnp.dot(w[:rows], low, preferred_element_type=jnp.float32)
    return both[:rows] + (both[rows:] + rest)


def scaled(value, angle):
    rank, width = angle.shape
    return (value.reshape(rank, SUB, width) * angle[:, None, :]).reshape(rank * SUB, width)


def kernel(
    chunks, rank, coeffs, phases, mixers, out, a, b, c_core, c_y, c_x, c_z, weights, cosines, z_cos,
    load_sem, core_send, core_recv, y_send, y_recv, x_send, x_recv, z_send, z_recv,
    back_send, back_recv, keep_sem, cos_send, cos_recv,
):
    wide, narrow = lax.axis_index("wide"), lax.axis_index("narrow")
    here = wide // 4
    core_peer, y_peer, x_peer = (wide, narrow ^ 1), (wide, narrow ^ 4), (wide ^ 2, narrow)
    z_peers = [(wide ^ (4 * p), narrow) for p in (1, 2, 3)]

    barrier = pltpu.get_barrier_semaphore()
    peers = [core_peer, y_peer, x_peer, *z_peers]
    for peer in peers:
        pl.semaphore_signal(barrier, inc=1, device_id=peer, device_id_type=MESH)
    pl.semaphore_wait(barrier, len(peers))

    def window(ref, k, q):
        group, part = k // SPLITS, k % SPLITS
        columns = pl.ds(pl.multiple_of(group * SUB, SUB), SUB)
        start = (q // 2) * 512 + part * (2 * WIDTH) + (q % 2) * WIDTH
        return ref.at[:, columns, pl.ds(pl.multiple_of(start, WIDTH), WIDTH)]

    def remote(src, dst, send, recv, peer):
        return pltpu.make_async_remote_copy(src, dst, send, recv, device_id=peer, device_id_type=MESH)

    def load(k, q):
        return pltpu.make_async_copy(window(coeffs, k, q), a.at[k, q], load_sem.at[k, q])

    def core_copy(k, q):
        return remote(window(coeffs, k, q), c_core.at[k, q], core_send.at[k, q], core_recv.at[k, q], core_peer)

    def y_copy(k):
        return remote(b.at[k], c_y.at[k], y_send.at[k], y_recv.at[k], y_peer)

    def x_copy(k):
        return remote(a.at[k], c_x.at[k], x_send.at[k], x_recv.at[k], x_peer)

    def z_copy(k, p):
        there = here ^ p
        return remote(b.at[k, there], c_z.at[k, here], z_send.at[k, p - 1], z_recv.at[k, p - 1], z_peers[p - 1])

    def back_copy(k, p):
        there = here ^ p
        return remote(a.at[k, there], window(out, k, here), back_send.at[k, p - 1], back_recv.at[k, p - 1], z_peers[p - 1])

    def keep_copy(k):
        return pltpu.make_async_copy(a.at[k, here], window(out, k, here), keep_sem.at[k])

    def cos_copy(p):
        there = here ^ p
        return remote(
            cosines.at[:, there, pl.ds(4, 2)], z_cos.at[here], cos_send.at[p - 1], cos_recv.at[p - 1], z_peers[p - 1]
        )

    def send_core(k, carry):
        for q in range(4):
            core_copy(k, q).start()
            load(k, q).start()
        return carry

    lax.fori_loop(0, chunks, send_core, 0)

    rows = rank * SUB

    def take_cosines(level):
        value = jnp.cos(phases[level])
        for part in range(SPLITS):
            for q in range(4):
                start = (q // 2) * 512 + part * (2 * WIDTH) + (q % 2) * WIDTH
                cosines[part, q, level] = value[:, start : start + WIDTH]

    spread = (
        lax.broadcasted_iota(jnp.int32, (2 * rank, 2 * rows), 0)
        == lax.broadcasted_iota(jnp.int32, (2 * rank, 2 * rows), 1) // SUB
    ).astype(jnp.bfloat16)
    same_column = (
        lax.broadcasted_iota(jnp.int32, (2 * rows, 2 * rows), 0) % SUB
        == lax.broadcasted_iota(jnp.int32, (2 * rows, 2 * rows), 1) % SUB
    )

    def take_weights(slot, level, side):
        mixer = jnp.concatenate([mixers[level, side, side], mixers[level, side, 1 - side]], axis=1)
        parts = [
            jnp.broadcast_to(part.astype(jnp.float32)[:, None, :], (rank, SUB, 2 * rank)).reshape(rows, 2 * rank)
            for part in split(mixer)
        ]
        tall = jnp.concatenate(parts, axis=0).astype(jnp.bfloat16)
        wide_values = jnp.dot(tall, spread, preferred_element_type=jnp.float32)
        weights[slot] = jnp.where(same_column, wide_values, 0.0).astype(jnp.bfloat16)

    for level in (4, 5):
        take_cosines(level)
    for p in (2, 1, 3):
        cos_copy(p).start()
    z_cos[here] = cosines[:, here, 4:6]
    take_cosines(0)
    take_weights(0, 0, narrow % 2)

    def pair(ref, k, first, second):
        return jnp.concatenate([ref[k, first].reshape(rows, WIDTH), ref[k, second].reshape(rows, WIDTH)], axis=1)

    def put(ref, k, first, second, value):
        ref[k, first] = value[:, :WIDTH].reshape(rank, SUB, WIDTH)
        ref[k, second] = value[:, WIDTH:].reshape(rank, SUB, WIDTH)

    def angles(k, level, half):
        part = k % SPLITS
        return jnp.concatenate([cosines[part, 2 * half, level], cosines[part, 2 * half + 1, level]], axis=1)

    def level_0(k):
        for q in range(4):
            core_copy(k, q).wait()
            load(k, q).wait()
        for half in range(2):
            at = (2 * half, 2 * half + 1)
            value = mixed(weights.at[0], pair(a, k, *at), pair(c_core, k, *at))
            put(b, k, *at, scaled(value, angles(k, 0, half)))
        y_copy(k).start()

    def levels_1_2(k):
        y_copy(k).wait_recv()
        between = []
        for half in range(2):
            at = (2 * half, 2 * half + 1)
            value = mixed(weights.at[1], pair(b, k, *at), pair(c_y, k, *at))
            between.append(scaled(value, angles(k, 1, half)))
        for half in range(2):
            value = mixed(weights.at[2 + half], between[half], between[1 - half])
            put(a, k, 2 * half, 2 * half + 1, scaled(value, angles(k, 2, half)))
        x_copy(k).start()

    def level_3(k):
        x_copy(k).wait_recv()
        y_copy(k).wait_send()
        for half in range(2):
            at = (2 * half, 2 * half + 1)
            value = mixed(weights.at[4], pair(a, k, *at), pair(c_x, k, *at))
            put(b, k, *at, scaled(value, angles(k, 3, half)))
        for p in (2, 1, 3):
            z_copy(k, p).start()
        c_z[k, here] = b[k, here]

    def levels_4_5(k):
        part = k % SPLITS
        for p in (1, 2, 3):
            z_copy(k, p).wait_recv()
        x_copy(k).wait_send()
        even, odd = pair(c_z, k, 0, 2), pair(c_z, k, 1, 3)

        def z_angles(level, first, second):
            return jnp.concatenate([z_cos[first, part, level], z_cos[second, part, level]], axis=1)

        even, odd = (
            scaled(mixed(weights.at[5], even, odd), z_angles(0, 0, 2)),
            scaled(mixed(weights.at[6], odd, even), z_angles(0, 1, 3)),
        )
        low = jnp.concatenate([even[:, :WIDTH], odd[:, :WIDTH]], axis=1)
        high = jnp.concatenate([even[:, WIDTH:], odd[:, WIDTH:]], axis=1)
        put(a, k, 0, 1, scaled(mixed(weights.at[7], low, high), z_angles(1, 0, 1)))
        put(a, k, 2, 3, scaled(mixed(weights.at[8], high, low), z_angles(1, 2, 3)))
        for p in (2, 1, 3):
            back_copy(k, p).start()
        keep_copy(k).start()

    ahead = 2
    level_0(0)
    take_cosines(1)
    take_weights(1, 1, narrow // 4)
    level_0(1)
    take_cosines(2)
    take_cosines(3)
    for slot, level, side in ((2, 2, 0), (3, 2, 1), (4, 3, wide // 2 % 2), (5, 4, 0), (6, 4, 1), (7, 5, 0), (8, 5, 1)):
        take_weights(slot, level, side)
    for p in (1, 2, 3):
        cos_copy(p).wait()

    def tick(t, carry):
        pl.when(t < chunks)(lambda: levels_1_2(t))
        pl.when(t + ahead < chunks)(lambda: level_0(t + ahead))
        pl.when(jnp.logical_and(t >= 1, t < chunks + 1))(lambda: level_3(t - 1))
        pl.when(jnp.logical_and(t >= 2, t < chunks + 2))(lambda: levels_4_5(t - 2))
        return carry

    lax.fori_loop(0, chunks + 2, tick, 0)

    def drain(k, carry):
        for p in (1, 2, 3):
            z_copy(k, p).wait_send()
            back_copy(k, p).wait()
        keep_copy(k).wait()
        return carry

    lax.fori_loop(0, chunks, drain, 0)


def on_device(coeffs, phases, mixers):
    rank, columns, blocks = coeffs.shape
    levels = phases.shape[0]
    chunks = columns // SUB * SPLITS
    piece = pltpu.VMEM((chunks, 4, rank, SUB, WIDTH), jnp.float32)
    dma = pltpu.SemaphoreType.DMA
    any_space = pl.BlockSpec(memory_space=pl.ANY)
    vmem = pl.BlockSpec(memory_space=pltpu.VMEM)
    return pl.pallas_call(
        functools.partial(kernel, chunks, rank),
        out_shape=jax.ShapeDtypeStruct(coeffs.shape, coeffs.dtype),
        in_specs=[any_space, vmem, vmem],
        out_specs=any_space,
        scratch_shapes=[
            piece, piece, piece, piece, piece, piece,
            pltpu.VMEM((9, 2 * rank * SUB, 2 * rank * SUB), jnp.bfloat16),
            pltpu.VMEM((SPLITS, 4, levels, rank, WIDTH), jnp.float32),
            pltpu.VMEM((4, SPLITS, 2, rank, WIDTH), jnp.float32),
            dma((chunks, 4)), dma((chunks, 4)), dma((chunks, 4)),
            dma((chunks,)), dma((chunks,)), dma((chunks,)), dma((chunks,)),
            dma((chunks, 3)), dma((chunks, 3)), dma((chunks, 3)), dma((chunks, 3)),
            dma((chunks,)), dma((3,)), dma((3,)),
        ],
        compiler_params=pltpu.CompilerParams(
            collective_id=0, has_side_effects=True, vmem_limit_bytes=60 * 2**20
        ),
    )(coeffs, phases, mixers)


def solution(mesh):
    placed = (P(None, None, ("wide", "narrow")), P(None, None, ("wide", "narrow")), P())
    return jax.shard_map(
        on_device,
        mesh=mesh,
        in_specs=placed,
        out_specs=P(None, None, ("wide", "narrow")),
        check_vma=False,
    )
```

time: 691 us -> 185 us (0.27)
  waiting for transfers between devices: 508 us -> 0 us
  Pallas kernels: 0 us -> 178 us
  matrix products: 108 us -> 0 us
  local copies, waits for them, and re-layouts: 58.3 us -> 6.61 us
  starting transfers between devices: 12.7 us -> 0 us
    ppermute x5 -> x0, waiting for transfers between devices: 508 us -> none  [swapped(): lax.ppermute(shard, axis, [(i, i ^ 1 << distance) for i in range(lax.axis...]
    pallas_call x0 -> x1, Pallas kernels: none -> 178 us  [on_device(): pl.pallas_call(functools.partial(kernel, chunks, rank), out_shape=jax.Sha...]
    dot_general x14 -> x0, matrix products: 108 us -> none  [the longest x5 46.4 us: paired_level(): jnp.einsum('ar,rcb->acb', mixing[side, 1 - side], partner, precision=lax....]
    reshape x3 -> x0, local copies, waits for them, and re-layouts: 27.1 us -> none  [the longest x2 17.8 us: combine_level(): return jnp.stack(outputs, axis=3).reshape(rank_size, col_size, total)]
    slice x3 -> x0, local copies, waits for them, and re-layouts: 13.6 us -> none  [the longest x1 12.9 us: combine_level(): second = shaped[:, :, :, 1, :]]
    ppermute x5 -> x0, starting transfers between devices: 12.7 us -> none  [swapped(): lax.ppermute(shard, axis, [(i, i ^ 1 << distance) for i in range(lax.axis...]
  transfers between devices with their start and end apart: 5 -> 0, of which waited for: 4 -> 0; matrix products, arithmetic and copies ran while one was open for 7% -> 0% of each run, Pallas kernels for 0% -> 0%
where the time goes in v1:
time: 185 us; the launch traced here: 184 us
  Pallas kernels  178 us (96%)
  local copies, waits for them, and re-layouts  6.61 us (4%)
    pallas_call x1, Pallas kernels, on_device(): pl.pallas_call(functools.partial(kernel, chunks, rank), out_shape=jax.Sha...  178 us
    unnamed x1, local copies, waits for them, and re-layouts  6.61 us

profile of v1, /device:TPU:0, one launch (start us, length us, event | category | flops | bytes accessed | tf_op | source)
XLA Modules:
  0.0 184.4 jit_solution(13738226902599930299)
XLA Ops:
  0.0 177.8 %shard_map.37 = f32[24,64,1024]{2,1,0:T(8,128)} custom-call(f32[24,64,1024]{2,1,0:T(8,128)} %coeffs.1, f32[6,24,1024]{2,1,0:T(8,128)} %phases.1, f32[6,2,2,24,24]{4,3,2,1,0:T(8,128)} %mixers.1), custom_call_target="tpu_custom_call" | custom-call | tf_op jit(solution)/shard_map/pallas_call | solution.py:240
  177.8 6.6 %copy.5 = f32[24,64,1024]{2,1,0:T(8,128)} copy(f32[24,64,1024]{2,1,0:T(8,128)} %shard_map.37) | data formatting | bytes 12582912

commit v2 on v1

v2 whole, which is shorter than its diff:
```python
import functools

import jax
import jax.numpy as jnp
from jax import lax
from jax.experimental import pallas as pl
from jax.experimental.pallas import tpu as pltpu
from jax.sharding import PartitionSpec as P

MESH = pl.DeviceIdType.MESH
SUB = 8
WIDTH = 128
AHEAD = 3
LAG_X = 2
LAG_Z = 4
FETCH = 4
ORDER = (2, 1, 3)


def split(x):
    high = x.astype(jnp.bfloat16)
    return high, (x - high.astype(jnp.float32)).astype(jnp.bfloat16)


def cosine(angle):
    half = 0.5 * angle
    square = half * half
    series = jnp.full_like(square, 1.0)
    for n in (12, 10, 8, 6, 4, 2):
        series = 1.0 - series * square * (1.0 / (n * (n + 1)))
    sine = half * series
    return 1.0 - 2.0 * sine * sine


def mixed(w, own, other):
    rows = own.shape[0]
    own_high, own_low = split(own)
    other_high, other_low = split(other)
    high = jnp.concatenate([own_high, other_high], axis=0)
    low = jnp.concatenate([own_low, other_low], axis=0)
    both = jnp.dot(w[...], high, preferred_element_type=jnp.float32)
    rest = jnp.dot(w[:rows], low, preferred_element_type=jnp.float32)
    return both[:rows] + (both[rows:] + rest)


def scaled(value, angle):
    rank, width = angle.shape
    return (value.reshape(rank, SUB, width) * angle[:, None, :]).reshape(rank * SUB, width)


def kernel(
    units, rank, coeffs, phases_in, mixers_in, out, a, b, c_core, c_y, c_x, c_z, phases, mixers, weights, cosines,
    z_cos, small_sem, load_sem, core_send, core_recv, y_send, y_recv, x_send, x_recv, z_send, z_recv,
    back_send, back_recv, keep_sem, cos_send, cos_recv,
):
    wide, narrow = lax.axis_index("wide"), lax.axis_index("narrow")
    here, column = wide // 4, wide % 4
    core_peer, y_peer, x_peer = (wide, narrow ^ 1), (wide, narrow ^ 4), (wide ^ 2, narrow)
    half_lanes = coeffs.shape[2] // 2
    rows = rank * SUB

    def z_device(there):
        return there * 4 + column, narrow

    barrier = pltpu.get_barrier_semaphore()
    peers = [core_peer, y_peer, x_peer, *(z_device(here ^ p) for p in ORDER)]
    for peer in peers:
        pl.semaphore_signal(barrier, inc=1, device_id=peer, device_id_type=MESH)

    def window(ref, group, half, tile):
        columns = pl.ds(pl.multiple_of(group * SUB, SUB), SUB)
        return ref.at[:, columns, pl.ds(pl.multiple_of(half * half_lanes + tile * WIDTH, WIDTH), WIDTH)]

    def remote(src, dst, send, recv, peer):
        return pltpu.make_async_remote_copy(src, dst, send, recv, device_id=peer, device_id_type=MESH)

    def load(k, half):
        return pltpu.make_async_copy(window(coeffs, k // 4, half, k % 4), a.at[k, half], load_sem.at[k, half])

    def core_copy(k, half):
        src = window(coeffs, k // 4, half, k % 4)
        return remote(src, c_core.at[k, half], core_send.at[k, half], core_recv.at[k, half], core_peer)

    def y_copy(k):
        return remote(b.at[k], c_y.at[k], y_send.at[k], y_recv.at[k], y_peer)

    def x_copy(k):
        return remote(a.at[k], c_x.at[k], x_send.at[k], x_recv.at[k], x_peer)

    def z_copy(k, half):
        there = 2 * half + k % 2
        return remote(b.at[k, half], c_z.at[k // 2, here], z_send.at[k, half], z_recv.at[k // 2, here], z_device(there))

    def z_arrival(s, there):
        return remote(b.at[2 * s, 0], c_z.at[s, there], z_send.at[2 * s, 0], z_recv.at[s, there], z_device(there))

    def back_copy(s, p):
        there = here ^ p
        src = a.at[2 * s + there // 2, there % 2]
        dst = window(out, s // 2, here // 2, 2 * (s % 2) + here % 2)
        return remote(src, dst, back_send.at[s, p - 1], back_recv.at[s, p - 1], z_device(there))

    def keep_copy(s):
        src = a.at[2 * s + here // 2, here % 2]
        return pltpu.make_async_copy(src, window(out, s // 2, here // 2, 2 * (s % 2) + here % 2), keep_sem.at[s])

    def cos_copy(p):
        there = here ^ p
        src = cosines.at[:, there % 2, there // 2, pl.ds(4, 2)]
        return remote(src, z_cos.at[here], cos_send.at[p - 1], cos_recv.at[p - 1], z_device(there))

    load_phases = pltpu.make_async_copy(phases_in, phases, small_sem.at[0])
    load_mixers = pltpu.make_async_copy(mixers_in, mixers, small_sem.at[1])
    load_mixers.start()
    load_phases.start()

    def fetch_own(k):
        for half in range(2):
            load(k, half).start()

    def fetch_core(k):
        for half in range(2):
            core_copy(k, half).start()

    for k in range(FETCH):
        fetch_own(k)

    def take_cosines(level):
        value = cosine(phases[level])
        for tile in range(4):
            for half in range(2):
                start = half * half_lanes + tile * WIDTH
                cosines[tile // 2, tile % 2, half, level] = value[:, start : start + WIDTH]

    spread = (
        lax.broadcasted_iota(jnp.int32, (2 * rank, 2 * rows), 0)
        == lax.broadcasted_iota(jnp.int32, (2 * rank, 2 * rows), 1) // SUB
    ).astype(jnp.bfloat16)
    same_column = (
        lax.broadcasted_iota(jnp.int32, (2 * rows, 2 * rows), 0) % SUB
        == lax.broadcasted_iota(jnp.int32, (2 * rows, 2 * rows), 1) % SUB
    )

    def take_weights(slot, level, side):
        mixer = jnp.concatenate([mixers[level, side, side], mixers[level, side, 1 - side]], axis=1)
        parts = [
            jnp.broadcast_to(part.astype(jnp.float32)[:, None, :], (rank, SUB, 2 * rank)).reshape(rows, 2 * rank)
            for part in split(mixer)
        ]
        tall = jnp.concatenate(parts, axis=0).astype(jnp.bfloat16)
        wide_values = jnp.dot(tall, spread, preferred_element_type=jnp.float32)
        weights[slot] = jnp.where(same_column, wide_values, 0.0).astype(jnp.bfloat16)

    load_mixers.wait()
    take_weights(0, 0, narrow % 2)
    load_phases.wait()
    take_cosines(0)
    pl.semaphore_wait(barrier, len(peers))
    for k in range(FETCH):
        fetch_core(k)
    take_weights(1, 1, narrow // 4)

    def both(ref, k):
        return jnp.concatenate([ref[k, 0].reshape(rows, WIDTH), ref[k, 1].reshape(rows, WIDTH)], axis=1)

    def put(ref, k, value):
        ref[k, 0] = value[:, :WIDTH].reshape(rank, SUB, WIDTH)
        ref[k, 1] = value[:, WIDTH:].reshape(rank, SUB, WIDTH)

    def angle(k, level, half):
        return cosines[k % 4 // 2, k % 2, half, level]

    def angles(k, level):
        return jnp.concatenate([angle(k, level, 0), angle(k, level, 1)], axis=1)

    def level_0(k):
        @pl.when(k + FETCH < units)
        def _():
            fetch_own(k + FETCH)
            fetch_core(k + FETCH)

        for half in range(2):
            core_copy(k, half).wait()
            load(k, half).wait()
        put(b, k, scaled(mixed(weights.at[0], both(a, k), both(c_core, k)), angles(k, 0)))
        y_copy(k).start()

    def levels_1_2(k):
        y_copy(k).wait_recv()
        value = scaled(mixed(weights.at[1], both(b, k), both(c_y, k)), angles(k, 1))
        low, high = value[:, :WIDTH], value[:, WIDTH:]
        a[k, 0] = scaled(mixed(weights.at[2], low, high), angle(k, 2, 0)).reshape(rank, SUB, WIDTH)
        a[k, 1] = scaled(mixed(weights.at[3], high, low), angle(k, 2, 1)).reshape(rank, SUB, WIDTH)
        x_copy(k).start()

    def level_3(k):
        x_copy(k).wait_recv()
        y_copy(k).wait_send()
        put(b, k, scaled(mixed(weights.at[4], both(a, k), both(c_x, k)), angles(k, 3)))
        for half in range(2):
            there = 2 * half + k % 2

            @pl.when(there != here)
            def _():
                z_copy(k, half).start()

            @pl.when(there == here)
            def _():
                c_z[k // 2, here] = b[k, half]

    def levels_4_5(s):
        for p in (1, 2, 3):
            z_arrival(s, here ^ p).wait_recv()
        x_copy(2 * s).wait_send()
        x_copy(2 * s + 1).wait_send()

        def z_pair(first, second):
            return jnp.concatenate([c_z[s, first].reshape(rows, WIDTH), c_z[s, second].reshape(rows, WIDTH)], axis=1)

        def z_angles(level, first, second):
            return jnp.concatenate([z_cos[first, s % 2, level], z_cos[second, s % 2, level]], axis=1)

        even, odd = z_pair(0, 2), z_pair(1, 3)
        even, odd = (
            scaled(mixed(weights.at[5], even, odd), z_angles(0, 0, 2)),
            scaled(mixed(weights.at[6], odd, even), z_angles(0, 1, 3)),
        )
        low = jnp.concatenate([even[:, :WIDTH], odd[:, :WIDTH]], axis=1)
        high = jnp.concatenate([even[:, WIDTH:], odd[:, WIDTH:]], axis=1)
        put(a, 2 * s, scaled(mixed(weights.at[7], low, high), z_angles(1, 0, 1)))
        put(a, 2 * s + 1, scaled(mixed(weights.at[8], high, low), z_angles(1, 2, 3)))
        for p in ORDER:
            back_copy(s, p).start()
        keep_copy(s).start()

    level_0(0)
    level_0(1)
    take_cosines(1)
    take_cosines(2)
    for slot, level, side in ((2, 2, 0), (3, 2, 1)):
        take_weights(slot, level, side)
    for level in (4, 5):
        take_cosines(level)
    for p in ORDER:
        cos_copy(p).start()
    z_cos[here] = cosines[:, here % 2, here // 2, 4:6]
    level_0(2)
    take_cosines(3)
    for slot, level, side in ((4, 3, wide // 2 % 2), (5, 4, 0), (6, 4, 1), (7, 5, 0), (8, 5, 1)):
        take_weights(slot, level, side)

    def tick(t, carry):
        levels_1_2(t)
        pl.when(t >= LAG_X)(lambda: level_3(t - LAG_X))
        pl.when(jnp.logical_and(t > LAG_Z, (t - LAG_Z) % 2 == 1))(lambda: levels_4_5((t - LAG_Z - 1) // 2))
        pl.when(t + AHEAD < units)(lambda: level_0(t + AHEAD))
        return carry

    def last(i, carry):
        level_3(units - 2 + i)
        levels_4_5(units // 2 - 2 + i)
        return carry

    lax.fori_loop(0, 4, tick, 0)
    for p in (1, 2, 3):
        cos_copy(p).wait()
    lax.fori_loop(4, units, tick, 0)
    lax.fori_loop(0, 2, last, 0)

    def drain(s, carry):
        for k in (2 * s, 2 * s + 1):
            for half in range(2):
                pl.when(2 * half + k % 2 != here)(z_copy(k, half).wait_send)
        for p in (1, 2, 3):
            back_copy(s, p).wait()
        keep_copy(s).wait()
        return carry

    lax.fori_loop(0, units // 2, drain, 0)


def on_device(coeffs, phases, mixers):
    rank, columns, blocks = coeffs.shape
    levels = phases.shape[0]
    units = columns // SUB * (blocks // (2 * WIDTH))

    piece = pltpu.VMEM((units, 2, rank, SUB, WIDTH), jnp.float32)
    dma = pltpu.SemaphoreType.DMA
    any_space = pl.BlockSpec(memory_space=pl.ANY)
    vmem = pl.BlockSpec(memory_space=pltpu.VMEM)
    return pl.pallas_call(
        functools.partial(kernel, units, rank),
        out_shape=pltpu.VMEM(coeffs.shape, coeffs.dtype),
        in_specs=[any_space, any_space, any_space],
        out_specs=vmem,
        scratch_shapes=[
            piece, piece, piece, piece, piece,
            pltpu.VMEM((units // 2, 4, rank, SUB, WIDTH), jnp.float32),
            pltpu.VMEM(phases.shape, jnp.float32),
            pltpu.VMEM(mixers.shape, jnp.float32),
            pltpu.VMEM((9, 2 * rank * SUB, 2 * rank * SUB), jnp.bfloat16),
            pltpu.VMEM((2, 2, 2, levels, rank, WIDTH), jnp.float32),
            pltpu.VMEM((4, 2, 2, rank, WIDTH), jnp.float32),
            dma((2,)), dma((units, 2)), dma((units, 2)), dma((units, 2)),
            dma((units,)), dma((units,)), dma((units,)), dma((units,)),
            dma((units, 2)), dma((units // 2, 4)), dma((units // 2, 3)), dma((units // 2, 3)),
            dma((units // 2,)), dma((3,)), dma((3,)),
        ],
        compiler_params=pltpu.CompilerParams(
            collective_id=0, has_side_effects=True, vmem_limit_bytes=48 * 2**20
        ),
    )(coeffs, phases, mixers)


def solution(mesh):
    placed = (P(None, None, ("wide", "narrow")), P(None, None, ("wide", "narrow")), P())
    return jax.shard_map(
        on_device,
        mesh=mesh,
        in_specs=placed,
        out_specs=P(None, None, ("wide", "narrow")),
        check_vma=False,
    )
```

time: 185 us -> 180 us (0.973)
  local copies, waits for them, and re-layouts: 6.61 us -> 2.71 us
    unnamed x1, local copies, waits for them, and re-layouts: 6.61 us -> 2.71 us
where the time goes in v2:
time: 180 us
  Pallas kernels  177 us (98%)
  local copies, waits for them, and re-layouts  2.71 us (2%)
    pallas_call x1, Pallas kernels, on_device(): pl.pallas_call(functools.partial(kernel, units, rank), out_shape=pltpu.VM...  177 us

profile of v2, /device:TPU:0, one launch (start us, length us, event | category | flops | bytes accessed | tf_op | source)
XLA Modules:
  0.0 179.9 jit_solution(4804124754991613474)
XLA Ops:
  0.0 177.2 %shard_map.37 = f32[24,64,1024]{2,1,0:T(8,128)S(1)} custom-call(f32[24,64,1024]{2,1,0:T(8,128)} %coeffs.1, f32[6,24,1024]{2,1,0:T(8,128)} %phases_in.1, f32[6,2,2,24,24]{4,3,2,1,0:T(8,128)} %mixers_in.1), custom_call_target="tpu_custom_call" | custom-call | tf_op jit(solution)/shard_map/pallas_call | solution.py:291
  177.2 2.7 %copy.5 = f32[24,64,1024]{2,1,0:T(8,128)} copy(f32[24,64,1024]{2,1,0:T(8,128)S(1)} %shard_map.37) | data formatting | bytes 12582912

commit v3 on v2

--- a/solution.py
+++ b/solution.py
@@ -11,10 +11,12 @@
 SUB = 8
 WIDTH = 128
 AHEAD = 3
-LAG_X = 2
-LAG_Z = 4
+LAG_X = 1
+LAG_Z = 3
+LAG_OUT = 5
 FETCH = 4
 ORDER = (2, 1, 3)
+QUARTER = WIDTH // 2
 
 
 def split(x):
@@ -33,7 +35,7 @@
 
 
 def mixed(w, own, other):
-    rows = own.shape[0]
+    rows = w.shape[0] // 2
     own_high, own_low = split(own)
     other_high, other_low = split(other)
     high = jnp.concatenate([own_high, other_high], axis=0)
@@ -43,15 +45,22 @@
     return both[:rows] + (both[rows:] + rest)
 
 
+def halves(first, second):
+    lane = lax.broadcasted_iota(jnp.int32, first.shape, first.ndim - 1)
+    near = lane < QUARTER
+    turn = functools.partial(pltpu.roll, shift=QUARTER, axis=first.ndim - 1)
+    return jnp.where(near, first, turn(second)), jnp.where(near, turn(first), second)
+
+
 def scaled(value, angle):
     rank, width = angle.shape
     return (value.reshape(rank, SUB, width) * angle[:, None, :]).reshape(rank * SUB, width)
 
 
 def kernel(
-    units, rank, coeffs, phases_in, mixers_in, out, a, b, c_core, c_y, c_x, c_z, phases, mixers, weights, cosines,
-    z_cos, small_sem, load_sem, core_send, core_recv, y_send, y_recv, x_send, x_recv, z_send, z_recv,
-    back_send, back_recv, keep_sem, cos_send, cos_recv,
+    units, rank, coeffs, phases_in, mixers_in, out, a, b, c_core, c_y, c_x, c_z, phases, mixers, weights, weights_two,
+    cosines, z_cos, z_scale, small_sem, load_sem, core_send, core_recv, y_send, y_recv, x_send, x_recv, z_send, z_recv,
+    back_send, back_recv, cos_send, cos_recv,
 ):
     wide, narrow = lax.axis_index("wide"), lax.axis_index("narrow")
     here, column = wide // 4, wide % 4
@@ -87,26 +96,22 @@
     def x_copy(k):
         return remote(a.at[k], c_x.at[k], x_send.at[k], x_recv.at[k], x_peer)
 
-    def z_copy(k, half):
-        there = 2 * half + k % 2
-        return remote(b.at[k, half], c_z.at[k // 2, here], z_send.at[k, half], z_recv.at[k // 2, here], z_device(there))
-
-    def z_arrival(s, there):
-        return remote(b.at[2 * s, 0], c_z.at[s, there], z_send.at[2 * s, 0], z_recv.at[s, there], z_device(there))
-
-    def back_copy(s, p):
+    def piece(ref, k, there):
+        return ref.at[k, there // 2, pl.ds(there % 2 * (rank // 2), rank // 2)]
+
+    def z_copy(k, p):
         there = here ^ p
-        src = a.at[2 * s + there // 2, there % 2]
-        dst = window(out, s // 2, here // 2, 2 * (s % 2) + here % 2)
-        return remote(src, dst, back_send.at[s, p - 1], back_recv.at[s, p - 1], z_device(there))
-
-    def keep_copy(s):
-        src = a.at[2 * s + here // 2, here % 2]
-        return pltpu.make_async_copy(src, window(out, s // 2, here // 2, 2 * (s % 2) + here % 2), keep_sem.at[s])
+        src, dst = piece(b, k, there), piece(c_z, k, here)
+        return remote(src, dst, z_send.at[k, p - 1], z_recv.at[k, p - 1], z_device(there))
+
+    def back_copy(k, p):
+        there = here ^ p
+        src, dst = piece(a, k, there), piece(c_core, k, here)
+        return remote(src, dst, back_send.at[k, p - 1], back_recv.at[k, p - 1], z_device(there))
 
     def cos_copy(p):
         there = here ^ p
-        src = cosines.at[:, there % 2, there // 2, pl.ds(4, 2)]
+        src = cosines.at[:, :, there // 2, pl.ds(4, 2)]
         return remote(src, z_cos.at[here], cos_send.at[p - 1], cos_recv.at[p - 1], z_device(there))
 
     load_phases = pltpu.make_async_copy(phases_in, phases, small_sem.at[0])
@@ -151,6 +156,17 @@
         wide_values = jnp.dot(tall, spread, preferred_element_type=jnp.float32)
         weights[slot] = jnp.where(same_column, wide_values, 0.0).astype(jnp.bfloat16)
 
+    def take_weights_two(slot, level):
+        mixer = jnp.concatenate(
+            [jnp.concatenate([mixers[level, side, 0], mixers[level, side, 1]], axis=1) for side in range(2)], axis=0
+        )
+        for at, part in enumerate(split(mixer)):
+            tall = jnp.broadcast_to(part.astype(jnp.float32)[:, None, :], (2 * rank, SUB, 2 * rank))
+            tall = tall.reshape(2 * rows, 2 * rank).astype(jnp.bfloat16)
+            wide_values = jnp.dot(tall, spread, preferred_element_type=jnp.float32)
+            values = jnp.where(same_column, wide_values, 0.0).astype(jnp.bfloat16)
+            weights_two[slot, at * 2 * rows : (at + 1) * 2 * rows] = values
+
     load_mixers.wait()
     take_weights(0, 0, narrow % 2)
     load_phases.wait()
@@ -188,95 +204,112 @@
     def levels_1_2(k):
         y_copy(k).wait_recv()
         value = scaled(mixed(weights.at[1], both(b, k), both(c_y, k)), angles(k, 1))
-        low, high = value[:, :WIDTH], value[:, WIDTH:]
-        a[k, 0] = scaled(mixed(weights.at[2], low, high), angle(k, 2, 0)).reshape(rank, SUB, WIDTH)
-        a[k, 1] = scaled(mixed(weights.at[3], high, low), angle(k, 2, 1)).reshape(rank, SUB, WIDTH)
+        value = mixed(weights_two.at[0], value[:, :WIDTH], value[:, WIDTH:])
+        for half in range(2):
+            part = scaled(value[half * rows : (half + 1) * rows], angle(k, 2, half))
+            a[k, half] = part.reshape(rank, SUB, WIDTH)
         x_copy(k).start()
+
+    def put_pieces(ref, k, half, tile):
+        first, second = halves(tile[: rank // 2], tile[rank // 2 :])
+        ref[k, half, : rank // 2] = first
+        ref[k, half, rank // 2 :] = second
+
+    def join(first, second):
+        return jnp.concatenate(halves(first, second), axis=0)
 
     def level_3(k):
         x_copy(k).wait_recv()
         y_copy(k).wait_send()
-        put(b, k, scaled(mixed(weights.at[4], both(a, k), both(c_x, k)), angles(k, 3)))
-        for half in range(2):
-            there = 2 * half + k % 2
-
-            @pl.when(there != here)
-            def _():
-                z_copy(k, half).start()
-
-            @pl.when(there == here)
-            def _():
-                c_z[k // 2, here] = b[k, half]
-
-    def levels_4_5(s):
+        value = scaled(mixed(weights.at[2], both(a, k), both(c_x, k)), angles(k, 3))
+        for half in range(2):
+            put_pieces(b, k, half, value[:, half * WIDTH : (half + 1) * WIDTH].reshape(rank, SUB, WIDTH))
+        for p in ORDER:
+            z_copy(k, p).start()
+        piece(c_z, k, here)[...] = piece(b, k, here)[...]
+
+    def levels_4_5(k):
         for p in (1, 2, 3):
-            z_arrival(s, here ^ p).wait_recv()
-        x_copy(2 * s).wait_send()
-        x_copy(2 * s + 1).wait_send()
-
-        def z_pair(first, second):
-            return jnp.concatenate([c_z[s, first].reshape(rows, WIDTH), c_z[s, second].reshape(rows, WIDTH)], axis=1)
-
-        def z_angles(level, first, second):
-            return jnp.concatenate([z_cos[first, s % 2, level], z_cos[second, s % 2, level]], axis=1)
-
-        even, odd = z_pair(0, 2), z_pair(1, 3)
-        even, odd = (
-            scaled(mixed(weights.at[5], even, odd), z_angles(0, 0, 2)),
-            scaled(mixed(weights.at[6], odd, even), z_angles(0, 1, 3)),
-        )
-        low = jnp.concatenate([even[:, :WIDTH], odd[:, :WIDTH]], axis=1)
-        high = jnp.concatenate([even[:, WIDTH:], odd[:, WIDTH:]], axis=1)
-        put(a, 2 * s, scaled(mixed(weights.at[7], low, high), z_angles(1, 0, 1)))
-        put(a, 2 * s + 1, scaled(mixed(weights.at[8], high, low), z_angles(1, 2, 3)))
+            z_copy(k, p).wait_recv()
+        x_copy(k).wait_send()
+
+        def z_piece(there):
+            return c_z[k, there // 2, there % 2 * (rank // 2) : (there % 2 + 1) * (rank // 2)]
+
+        def scale(n):
+            return z_scale[k % 4 // 2, k % 2, n]
+
+        even, odd = join(z_piece(0), z_piece(2)), join(z_piece(1), z_piece(3))
+        value = mixed(weights_two.at[1], even.reshape(rows, WIDTH), odd.reshape(rows, WIDTH))
+        low, high = halves(scaled(value[:rows], scale(0)), scaled(value[rows:], scale(1)))
+        value = mixed(weights_two.at[2], low, high)
+        for half in range(2):
+            tile = scaled(value[half * rows : (half + 1) * rows], scale(2 + half))
+            put_pieces(a, k, half, tile.reshape(rank, SUB, WIDTH))
         for p in ORDER:
-            back_copy(s, p).start()
-        keep_copy(s).start()
+            back_copy(k, p).start()
+        piece(c_core, k, here)[...] = piece(a, k, here)[...]
+
+    def result(k):
+        for p in (1, 2, 3):
+            back_copy(k, p).wait()
+            z_copy(k, p).wait_send()
+        for half in range(2):
+            tile = join(c_core[k, half, : rank // 2], c_core[k, half, rank // 2 :])
+            window(out, k // 4, half, k % 4)[...] = tile
+
+    def take_z_scale():
+        side = here % 2
+        for tile in range(4):
+            for level, pairs in enumerate((((0, 2), (1, 3)), ((0, 1), (2, 3)))):
+                for at, pair in enumerate(pairs):
+                    first, second = (z_cos[there, tile // 2, tile % 2, level] for there in pair)
+                    near, far = halves(first, second)
+                    z_scale[tile // 2, tile % 2, 2 * level + at] = jnp.where(side == 0, near, far)
 
     level_0(0)
     level_0(1)
     take_cosines(1)
     take_cosines(2)
-    for slot, level, side in ((2, 2, 0), (3, 2, 1)):
-        take_weights(slot, level, side)
+    take_weights_two(0, 2)
     for level in (4, 5):
         take_cosines(level)
     for p in ORDER:
         cos_copy(p).start()
-    z_cos[here] = cosines[:, here % 2, here // 2, 4:6]
+    z_cos[here] = cosines[:, :, here // 2, 4:6]
     level_0(2)
     take_cosines(3)
-    for slot, level, side in ((4, 3, wide // 2 % 2), (5, 4, 0), (6, 4, 1), (7, 5, 0), (8, 5, 1)):
-        take_weights(slot, level, side)
+    take_weights(2, 3, wide // 2 % 2)
+    take_weights_two(1, 4)
+    take_weights_two(2, 5)
+
+    def finish(t):
+        pl.when(t >= LAG_Z)(lambda: levels_4_5(t - LAG_Z))
+        pl.when(t >= LAG_OUT)(lambda: result(t - LAG_OUT))
 
     def tick(t, carry):
         levels_1_2(t)
+        finish(t)
+        pl.when(t + AHEAD < units)(lambda: level_0(t + AHEAD))
         pl.when(t >= LAG_X)(lambda: level_3(t - LAG_X))
-        pl.when(jnp.logical_and(t > LAG_Z, (t - LAG_Z) % 2 == 1))(lambda: levels_4_5((t - LAG_Z - 1) // 2))
-        pl.when(t + AHEAD < units)(lambda: level_0(t + AHEAD))
         return carry
 
-    def last(i, carry):
-        level_3(units - 2 + i)
-        levels_4_5(units // 2 - 2 + i)
+    def last(t, carry):
+        finish(t)
+        pl.when(t < units + LAG_X)(lambda: level_3(t - LAG_X))
         return carry
 
-    lax.fori_loop(0, 4, tick, 0)
+    def very_last(k, carry):
+        result(k)
+        return carry
+
+    lax.fori_loop(0, LAG_Z, tick, 0)
     for p in (1, 2, 3):
         cos_copy(p).wait()
-    lax.fori_loop(4, units, tick, 0)
-    lax.fori_loop(0, 2, last, 0)
-
-    def drain(s, carry):
-        for k in (2 * s, 2 * s + 1):
-            for half in range(2):
-                pl.when(2 * half + k % 2 != here)(z_copy(k, half).wait_send)
-        for p in (1, 2, 3):
-            back_copy(s, p).wait()
-        keep_copy(s).wait()
-        return carry
-
-    lax.fori_loop(0, units // 2, drain, 0)
+    take_z_scale()
+    lax.fori_loop(LAG_Z, units, tick, 0)
+    lax.fori_loop(units, units + LAG_Z, last, 0)
+    lax.fori_loop(units + LAG_Z - LAG_OUT, units, very_last, 0)
 
 
 def on_device(coeffs, phases, mixers):
@@ -294,17 +327,18 @@
         in_specs=[any_space, any_space, any_space],
         out_specs=vmem,
         scratch_shapes=[
-            piece, piece, piece, piece, piece,
-            pltpu.VMEM((units // 2, 4, rank, SUB, WIDTH), jnp.float32),
+            piece, piece, piece, piece, piece, piece,
             pltpu.VMEM(phases.shape, jnp.float32),
             pltpu.VMEM(mixers.shape, jnp.float32),
-            pltpu.VMEM((9, 2 * rank * SUB, 2 * rank * SUB), jnp.bfloat16),
+            pltpu.VMEM((3, 2 * rank * SUB, 2 * rank * SUB), jnp.bfloat16),
+            pltpu.VMEM((3, 4 * rank * SUB, 2 * rank * SUB), jnp.bfloat16),
             pltpu.VMEM((2, 2, 2, levels, rank, WIDTH), jnp.float32),
-            pltpu.VMEM((4, 2, 2, rank, WIDTH), jnp.float32),
+            pltpu.VMEM((4, 2, 2, 2, rank, WIDTH), jnp.float32),
+            pltpu.VMEM((2, 2, 4, rank, WIDTH), jnp.float32),
             dma((2,)), dma((units, 2)), dma((units, 2)), dma((units, 2)),
             dma((units,)), dma((units,)), dma((units,)), dma((units,)),
-            dma((units, 2)), dma((units // 2, 4)), dma((units // 2, 3)), dma((units // 2, 3)),
-            dma((units // 2,)), dma((3,)), dma((3,)),
+            dma((units, 3)), dma((units, 3)), dma((units, 3)), dma((units, 3)),
+            dma((3,)), dma((3,)),
         ],
         compiler_params=pltpu.CompilerParams(
             collective_id=0, has_side_effects=True, vmem_limit_bytes=48 * 2**20

time: 180 us -> 174 us (0.967)
  Pallas kernels: 177 us -> 171 us
    pallas_call x1, Pallas kernels: 177 us -> 171 us  [on_device(): pl.pallas_call(functools.partial(kernel, units, rank), out_shape=pltpu.VM...]
where the time goes in v3:
time: 174 us
  Pallas kernels  171 us (98%)
  local copies, waits for them, and re-layouts  2.71 us (2%)
    pallas_call x1, Pallas kernels, on_device(): pl.pallas_call(functools.partial(kernel, units, rank), out_shape=pltpu.VM...  171 us

profile of v3, /device:TPU:0, one launch (start us, length us, event | category | flops | bytes accessed | tf_op | source)
XLA Modules:
  0.0 173.8 jit_solution(12214521906206294080)
XLA Ops:
  0.0 171.1 %shard_map.37 = f32[24,64,1024]{2,1,0:T(8,128)S(1)} custom-call(f32[24,64,1024]{2,1,0:T(8,128)} %coeffs.1, f32[6,24,1024]{2,1,0:T(8,128)} %phases_in.1, f32[6,2,2,24,24]{4,3,2,1,0:T(8,128)} %mixers_in.1), custom_call_target="tpu_custom_call" | custom-call | tf_op jit(solution)/shard_map/pallas_call | solution.py:324
  171.1 2.7 %copy.5 = f32[24,64,1024]{2,1,0:T(8,128)} copy(f32[24,64,1024]{2,1,0:T(8,128)S(1)} %shard_map.37) | data formatting | bytes 12582912

commit v4 on v3

--- a/solution.py
+++ b/solution.py
@@ -14,7 +14,8 @@
 LAG_X = 1
 LAG_Z = 3
 LAG_OUT = 5
-FETCH = 4
+FETCH = 8
+SHARE = 4
 ORDER = (2, 1, 3)
 QUARTER = WIDTH // 2
 
@@ -86,9 +87,8 @@
     def load(k, half):
         return pltpu.make_async_copy(window(coeffs, k // 4, half, k % 4), a.at[k, half], load_sem.at[k, half])
 
-    def core_copy(k, half):
-        src = window(coeffs, k // 4, half, k % 4)
-        return remote(src, c_core.at[k, half], core_send.at[k, half], core_recv.at[k, half], core_peer)
+    def core_copy(k):
+        return remote(a.at[k], c_core.at[k], core_send.at[k], core_recv.at[k], core_peer)
 
     def y_copy(k):
         return remote(b.at[k], c_y.at[k], y_send.at[k], y_recv.at[k], y_peer)
@@ -123,12 +123,16 @@
         for half in range(2):
             load(k, half).start()
 
-    def fetch_core(k):
-        for half in range(2):
-            core_copy(k, half).start()
+    def share(k):
+        for half in range(2):
+            load(k, half).wait()
+        core_copy(k).start()
 
     for k in range(FETCH):
         fetch_own(k)
+    pl.semaphore_wait(barrier, len(peers))
+    for k in range(SHARE):
+        share(k)
 
     def take_cosines(level):
         value = cosine(phases[level])
@@ -171,10 +175,6 @@
     take_weights(0, 0, narrow % 2)
     load_phases.wait()
     take_cosines(0)
-    pl.semaphore_wait(barrier, len(peers))
-    for k in range(FETCH):
-        fetch_core(k)
-    take_weights(1, 1, narrow // 4)
 
     def both(ref, k):
         return jnp.concatenate([ref[k, 0].reshape(rows, WIDTH), ref[k, 1].reshape(rows, WIDTH)], axis=1)
@@ -190,14 +190,9 @@
         return jnp.concatenate([angle(k, level, 0), angle(k, level, 1)], axis=1)
 
     def level_0(k):
-        @pl.when(k + FETCH < units)
-        def _():
-            fetch_own(k + FETCH)
-            fetch_core(k + FETCH)
-
-        for half in range(2):
-            core_copy(k, half).wait()
-            load(k, half).wait()
+        pl.when(k + FETCH < units)(lambda: fetch_own(k + FETCH))
+        pl.when(k + SHARE < units)(lambda: share(k + SHARE))
+        core_copy(k).wait()
         put(b, k, scaled(mixed(weights.at[0], both(a, k), both(c_core, k)), angles(k, 0)))
         y_copy(k).start()
 
@@ -268,20 +263,28 @@
                     z_scale[tile // 2, tile % 2, 2 * level + at] = jnp.where(side == 0, near, far)
 
     level_0(0)
+    take_weights(1, 1, narrow // 4)
+    take_cosines(1)
     level_0(1)
-    take_cosines(1)
     take_cosines(2)
     take_weights_two(0, 2)
-    for level in (4, 5):
-        take_cosines(level)
-    for p in ORDER:
-        cos_copy(p).start()
-    z_cos[here] = cosines[:, :, here // 2, 4:6]
     level_0(2)
-    take_cosines(3)
-    take_weights(2, 3, wide // 2 % 2)
-    take_weights_two(1, 4)
-    take_weights_two(2, 5)
+
+    def before_level_3():
+        take_cosines(3)
+        take_weights(2, 3, wide // 2 % 2)
+        for level in (4, 5):
+            take_cosines(level)
+        for p in ORDER:
+            cos_copy(p).start()
+        z_cos[here] = cosines[:, :, here // 2, 4:6]
+
+    def before_level_5():
+        take_weights_two(1, 4)
+        take_weights_two(2, 5)
+        for p in (1, 2, 3):
+            cos_copy(p).wait()
+        take_z_scale()
 
     def finish(t):
         pl.when(t >= LAG_Z)(lambda: levels_4_5(t - LAG_Z))
@@ -292,6 +295,8 @@
         finish(t)
         pl.when(t + AHEAD < units)(lambda: level_0(t + AHEAD))
         pl.when(t >= LAG_X)(lambda: level_3(t - LAG_X))
+        pl.when(t == 0)(before_level_3)
+        pl.when(t == LAG_Z - 1)(before_level_5)
         return carry
 
     def last(t, carry):
@@ -303,11 +308,7 @@
         result(k)
         return carry
 
-    lax.fori_loop(0, LAG_Z, tick, 0)
-    for p in (1, 2, 3):
-        cos_copy(p).wait()
-    take_z_scale()
-    lax.fori_loop(LAG_Z, units, tick, 0)
+    lax.fori_loop(0, units, tick, 0)
     lax.fori_loop(units, units + LAG_Z, last, 0)
     lax.fori_loop(units + LAG_Z - LAG_OUT, units, very_last, 0)
 
@@ -335,7 +336,7 @@
             pltpu.VMEM((2, 2, 2, levels, rank, WIDTH), jnp.float32),
             pltpu.VMEM((4, 2, 2, 2, rank, WIDTH), jnp.float32),
             pltpu.VMEM((2, 2, 4, rank, WIDTH), jnp.float32),
-            dma((2,)), dma((units, 2)), dma((units, 2)), dma((units, 2)),
+            dma((2,)), dma((units, 2)), dma((units,)), dma((units,)),
             dma((units,)), dma((units,)), dma((units,)), dma((units,)),
             dma((units, 3)), dma((units, 3)), dma((units, 3)), dma((units, 3)),
             dma((3,)), dma((3,)),

time: 174 us -> 173 us (level)
  no operation moved by 1% of the time
where the time goes in v4:
time: 173 us
  Pallas kernels  170 us (98%)
  local copies, waits for them, and re-layouts  2.71 us (2%)
    pallas_call x1, Pallas kernels, on_device(): pl.pallas_call(functools.partial(kernel, units, rank), out_shape=pltpu.VM...  170 us

profile of v4, /device:TPU:0, one launch (start us, length us, event | category | flops | bytes accessed | tf_op | source)
XLA Modules:
  0.0 173.2 jit_solution(3218175344818225360)
XLA Ops:
  0.0 170.5 %shard_map.37 = f32[24,64,1024]{2,1,0:T(8,128)S(1)} custom-call(f32[24,64,1024]{2,1,0:T(8,128)} %coeffs.1, f32[6,24,1024]{2,1,0:T(8,128)} %phases_in.1, f32[6,2,2,24,24]{4,3,2,1,0:T(8,128)} %mixers_in.1), custom_call_target="tpu_custom_call" | custom-call | tf_op jit(solution)/shard_map/pallas_call | solution.py:325
  170.5 2.7 %copy.5 = f32[24,64,1024]{2,1,0:T(8,128)} copy(f32[24,64,1024]{2,1,0:T(8,128)S(1)} %shard_map.37) | data formatting | bytes 12582912

commit v5 on v4

--- a/solution.py
+++ b/solution.py
@@ -313,6 +313,18 @@
     lax.fori_loop(units + LAG_Z - LAG_OUT, units, very_last, 0)
 
 
+def write_out(parts, held, out, sems):
+    depth = held.shape[0] // parts
+    copies = [
+        pltpu.make_async_copy(held.at[pl.ds(n * depth, depth)], out.at[pl.ds(n * depth, depth)], sems.at[n])
+        for n in range(parts)
+    ]
+    for copy in copies:
+        copy.start()
+    for copy in copies:
+        copy.wait()
+
+
 def on_device(coeffs, phases, mixers):
     rank, columns, blocks = coeffs.shape
     levels = phases.shape[0]
@@ -322,7 +334,7 @@
     dma = pltpu.SemaphoreType.DMA
     any_space = pl.BlockSpec(memory_space=pl.ANY)
     vmem = pl.BlockSpec(memory_space=pltpu.VMEM)
-    return pl.pallas_call(
+    held = pl.pallas_call(
         functools.partial(kernel, units, rank),
         out_shape=pltpu.VMEM(coeffs.shape, coeffs.dtype),
         in_specs=[any_space, any_space, any_space],
@@ -345,6 +357,14 @@
             collective_id=0, has_side_effects=True, vmem_limit_bytes=48 * 2**20
         ),
     )(coeffs, phases, mixers)
+    return pl.pallas_call(
+        functools.partial(write_out, 8),
+        out_shape=jax.ShapeDtypeStruct(coeffs.shape, coeffs.dtype),
+        in_specs=[any_space],
+        out_specs=any_space,
+        scratch_shapes=[dma((8,))],
+        compiler_params=pltpu.CompilerParams(vmem_limit_bytes=2**20),
+    )(held)
 
 
 def solution(mesh):

time: 173 us -> 173 us (level)
  Pallas kernels: 170 us -> 173 us
  local copies, waits for them, and re-layouts: 2.71 us -> 0 us
    pallas_call x0 -> x1, Pallas kernels: none -> 2.74 us  [on_device(): pl.pallas_call(functools.partial(write_out, 8), out_shape=jax.ShapeDtypeS...]
    unnamed x1 -> x0, local copies, waits for them, and re-layouts: 2.71 us -> none
where the time goes in v5:
time: 173 us
  Pallas kernels  173 us (100%)
    pallas_call x1, Pallas kernels, on_device(): pl.pallas_call(functools.partial(kernel, units, rank), out_shape=pltpu.VM...  170 us

profile of v5, /device:TPU:0, one launch (start us, length us, event | category | flops | bytes accessed | tf_op | source)
XLA Modules:
  0.0 173.2 jit_solution(10288390781615326850)
XLA Ops:
  0.0 170.5 %shard_map.37.held = f32[24,64,1024]{2,1,0:T(8,128)S(1)} custom-call(f32[24,64,1024]{2,1,0:T(8,128)} %coeffs.1, f32[6,24,1024]{2,1,0:T(8,128)} %phases_in.1, f32[6,2,2,24,24]{4,3,2,1,0:T(8,128)} %mixers_in.1), custom_call_target="tpu_custom_call" | custom-call | tf_op jit(solution)/shard_map/pallas_call | solution.py:337
  170.5 2.7 %shard_map.38 = f32[24,64,1024]{2,1,0:T(8,128)} custom-call(f32[24,64,1024]{2,1,0:T(8,128)S(1)} %shard_map.37.held), custom_call_target="tpu_custom_call" | custom-call | tf_op jit(solution)/shard_map/pallas_call | solution.py:360
